TPU v7x, 32 devices: a whole 2x2x4 slice. The times are simulated.
32 devices in a mesh: ctx: 8 (over y, x, core), tp: 4 (over z).
Axes of the slice: x: 2, y: 2, z: 4, core: 2. Of those that a mesh axis runs over, the one named last changes fastest.
Arguments:
- tokens: bfloat16 [8, 1024, 768], P(None, 'ctx'), may hold values from -6 to 6
- cotangent: bfloat16 [8, 1024, 768], P(None, 'ctx'), may hold values from -1.5 to 1.5
- seq_lengths: int32 [8], replicated, may hold values from 256 to 1024, as said below
- combined_weight: bfloat16 [2, 768, 12, 3, 64], P(None, None, 'tp'), may hold values from -0.21875 to 0.21875
- joined_bias: bfloat16 [2, 12, 2, 64], P(None, 'tp'), may hold values from -3 to 3
- attention_out_weight: bfloat16 [2, 768, 768], P(None, 'tp'), may hold values from -9 to 9
- attention_out_bias: bfloat16 [2, 768], replicated, may hold values from -3 to 3
- expand_weight: bfloat16 [2, 768, 3072], P(None, None, 'tp'), may hold values from -0.21875 to 0.21875
- expand_bias: bfloat16 [2, 3072], P(None, 'tp'), may hold values from -3 to 3
- contract_weight: bfloat16 [2, 3072, 768], P(None, 'tp'), may hold values from -0.109375 to 0.109375
- contract_bias: bfloat16 [2, 768], replicated, may hold values from -3 to 3
- norm_gains: bfloat16 [2, 2, 768], replicated, may hold values from 0.25 to 1.75
- norm_shifts: bfloat16 [2, 2, 768], replicated, may hold values from -3 to 3
Outputs:
- outputs: float32 [8, 1024, 768], P(None, 'ctx')
- tokens_grad: float32 [8, 1024, 768], P(None, 'ctx')
- grad_joined: float32 [2, 768, 12, 3, 64], P(None, None, 'tp')
- grad_qvbias: float32 [2, 12, 2, 64], P(None, 'tp')
- grad_mixer: float32 [2, 768, 768], P(None, 'tp')
- grad_mbias: float32 [2, 768], replicated
- grad_upward: float32 [2, 768, 3072], P(None, None, 'tp')
- grad_ubias: float32 [2, 3072], P(None, 'tp')
- grad_down: float32 [2, 3072, 768], P(None, 'tp')
- grad_dbias: float32 [2, 768], replicated
- grad_gains: float32 [2, 2, 768], replicated
- grad_shifts: float32 [2, 2, 768], replicated
Inputs may be any that keep to these rules, and one draw needn't show every extreme that they name: `seq_lengths`: at least one sequence has length 1024 in every draw.
All inputs are finite; a program needn't handle non-finite values.
Results may differ from a plain program's by a relative error of at most 0.018.
Values may be sent and summed in bfloat16 or wider, within the bound.
A program may use at most 448 MiB of HBM per device.

v0:
```python
import jax
import jax.numpy as jnp
from jax import lax
from jax.sharding import PartitionSpec as P

EPS = 1e-12
MASKED = -1e30


def normalize(resid, norm_gain, norm_shift):
    row_mean = jnp.mean(resid, axis=-1, keepdims=True)
    centred = resid - row_mean
    spread = jnp.mean(centred * centred, axis=-1, keepdims=True)
    return centred * lax.rsqrt(spread + EPS) * norm_gain + norm_shift


def smooth_gate(value):
    return (
        0.5
        * value
        * (1.0 + jnp.tanh(0.7978845608028654 * (value + 0.044715 * value * value * value)))
    )


def attention_scores(queries, key_rows, key_valid, scale):
    scores = (
        jnp.einsum("sqhd,skhd->shqk", queries, key_rows, preferred_element_type=jnp.float32) * scale
    )
    return jnp.where(key_valid[:, None, None, :], scores, MASKED)


def share_sum(partial_rows):
    return lax.psum_scatter(partial_rows, "tp", scatter_dimension=1, tiled=True)


def share_gather(rows_low):
    return lax.all_gather(rows_low, "tp", axis=1, tiled=True)


def take_share(full_rows):
    share_rows = full_rows.shape[1] // lax.axis_size("tp")
    return lax.dynamic_slice_in_dim(full_rows, lax.axis_index("tp") * share_rows, share_rows, 1)


def forward_layer(
    hidden,
    hidden_reduced,
    seq_lengths,
    combined_weight,
    joined_bias,
    attention_out_weight,
    attention_out_bias,
    expand_weight,
    expand_bias,
    contract_weight,
    contract_bias,
    norm_gains,
    norm_shifts,
):
    n_seqs, n_rows, width = hidden_reduced.shape
    n_heads = combined_weight.shape[1]
    head_dim = combined_weight.shape[3]
    scale = head_dim ** (-0.5)
    joined_flat = combined_weight.reshape(width, -1)
    combined_projected = jnp.einsum(
        "sbd,dc->sbc", hidden_reduced, joined_flat, preferred_element_type=jnp.float32
    )
    combined_projected = combined_projected.reshape(n_seqs, n_rows, n_heads, 3, head_dim)
    queries = (combined_projected[..., 0, :] + joined_bias[:, 0, :]).astype(jnp.bfloat16)
    key_rows = combined_projected[..., 1, :].astype(jnp.bfloat16)
    value_rows = (combined_projected[..., 2, :] + joined_bias[:, 1, :]).astype(jnp.bfloat16)
    all_keys, all_values = (
        lax.all_gather(key_rows.reshape(n_seqs, n_rows, -1), "ctx", axis=1, tiled=True),
        lax.all_gather(value_rows.reshape(n_seqs, n_rows, -1), "ctx", axis=1, tiled=True),
    )
    total_len = all_keys.shape[1]
    all_keys = all_keys.reshape(n_seqs, total_len, n_heads, head_dim)
    all_values = all_values.reshape(n_seqs, total_len, n_heads, head_dim)
    key_valid = jnp.arange(total_len)[None, :] < seq_lengths[:, None]
    scores = attention_scores(queries, all_keys, key_valid, scale)
    row_max = jnp.max(scores, axis=-1, keepdims=True)
    log_total = row_max + jnp.log(jnp.sum(jnp.exp(scores - row_max), axis=-1, keepdims=True))
    attn_probs = jnp.exp(scores - log_total).astype(jnp.bfloat16)
    merged_head_output = jnp.einsum(
        "shqk,skhd->sqhd", attn_probs, all_values, preferred_element_type=jnp.float32
    )
    merged_head_output = merged_head_output.astype(jnp.bfloat16).reshape(n_seqs, n_rows, -1)
    attention_branch = jnp.einsum(
        "sbc,cd->sbd", merged_head_output, attention_out_weight, preferred_element_type=jnp.float32
    )
    attention_branch = share_sum(attention_branch)
    normalized_rows, first_back = jax.vjp(
        normalize, hidden + attention_branch + attention_out_bias, norm_gains[0], norm_shifts[0]
    )
    normed_low = normalized_rows.astype(jnp.bfloat16)
    normed_low = share_gather(normed_low)
    before_activation = (
        jnp.einsum("sbd,df->sbf", normed_low, expand_weight, preferred_element_type=jnp.float32)
        + expand_bias
    )
    activated_hidden, gate_back = jax.vjp(smooth_gate, before_activation)
    gated_low = activated_hidden.astype(jnp.bfloat16)
    feedforward_branch = jnp.einsum(
        "sbf,fd->sbd", gated_low, contract_weight, preferred_element_type=jnp.float32
    )
    feedforward_branch = share_sum(feedforward_branch)
    result, second_back = jax.vjp(
        normalize,
        normalized_rows + feedforward_branch + contract_bias,
        norm_gains[1],
        norm_shifts[1],
    )
    kept = (
        hidden_reduced,
        queries,
        key_rows,
        value_rows,
        all_keys,
        all_values,
        key_valid,
        log_total,
        merged_head_output,
        normed_low,
        gated_low,
        first_back,
        gate_back,
        second_back,
    )
    return (result, kept)


def backward_layer(
    grad_out, kept, combined_weight, attention_out_weight, expand_weight, contract_weight
):
    (
        hidden_reduced,
        queries,
        key_rows,
        value_rows,
        all_keys,
        all_values,
        key_valid,
        log_total,
        merged_head_output,
        normed_low,
        gated_low,
        first_back,
        gate_back,
        second_back,
    ) = kept
    n_seqs, n_rows, n_heads, head_dim = queries.shape
    width = hidden_reduced.shape[2]
    total_len = all_keys.shape[1]
    scale = head_dim ** (-0.5)
    d_resid_two, d_gain_two, d_shift_two = second_back(grad_out)
    d_down_bias = jnp.sum(d_resid_two, axis=(0, 1))
    d_branch_two = d_resid_two.astype(jnp.bfloat16)
    d_branch_two = share_gather(d_branch_two)
    d_down = jnp.einsum("sbf,sbd->fd", gated_low, d_branch_two, preferred_element_type=jnp.float32)
    d_gated = jnp.einsum(
        "sbd,fd->sbf", d_branch_two, contract_weight, preferred_element_type=jnp.float32
    )
    d_pre_gate = gate_back(d_gated)[0].astype(jnp.bfloat16)
    d_up_bias = jnp.sum(d_pre_gate.astype(jnp.float32), axis=(0, 1))
    d_upward = jnp.einsum("sbd,sbf->df", normed_low, d_pre_gate, preferred_element_type=jnp.float32)
    d_normed = jnp.einsum(
        "sbf,df->sbd", d_pre_gate, expand_weight, preferred_element_type=jnp.float32
    )
    d_normed = share_sum(d_normed) + d_resid_two
    d_resid_one, d_gain_one, d_shift_one = first_back(d_normed)
    d_mixer_bias = jnp.sum(d_resid_one, axis=(0, 1))
    d_branch = d_resid_one.astype(jnp.bfloat16)
    d_branch = share_gather(d_branch)
    d_mixer = jnp.einsum(
        "sbc,sbd->cd", merged_head_output, d_branch, preferred_element_type=jnp.float32
    )
    d_mixed = jnp.einsum(
        "sbd,cd->sbc", d_branch, attention_out_weight, preferred_element_type=jnp.float32
    )
    d_mixed = d_mixed.astype(jnp.bfloat16).reshape(n_seqs, n_rows, n_heads, head_dim)
    scores = attention_scores(queries, all_keys, key_valid, scale)
    probs_full = jnp.exp(scores - log_total)
    d_probs = jnp.einsum("sqhd,skhd->shqk", d_mixed, all_values, preferred_element_type=jnp.float32)
    row_delta = jnp.sum(probs_full * d_probs, axis=-1, keepdims=True)
    d_scores = (probs_full * (d_probs - row_delta)).astype(jnp.bfloat16)
    d_queries = (
        jnp.einsum("shqk,skhd->sqhd", d_scores, all_keys, preferred_element_type=jnp.float32)
        * scale
    )
    d_queries = d_queries.astype(jnp.bfloat16)
    key_part = (
        jnp.einsum("shqk,sqhd->skhd", d_scores, queries, preferred_element_type=jnp.float32) * scale
    )
    value_part = jnp.einsum(
        "shqk,sqhd->skhd",
        probs_full.astype(jnp.bfloat16),
        d_mixed,
        preferred_element_type=jnp.float32,
    )
    d_keys, d_values = (
        lax.psum_scatter(
            key_part.reshape(n_seqs, total_len, -1), "ctx", scatter_dimension=1, tiled=True
        ),
        lax.psum_scatter(
            value_part.reshape(n_seqs, total_len, -1), "ctx", scatter_dimension=1, tiled=True
        ),
    )
    d_keys = d_keys.reshape(n_seqs, n_rows, n_heads, head_dim)
    d_values = d_values.reshape(n_seqs, n_rows, n_heads, head_dim)
    d_keys = d_keys.astype(jnp.bfloat16)
    d_values = d_values.astype(jnp.bfloat16)
    d_joined_bias = jnp.stack(
        [
            jnp.sum(d_queries.astype(jnp.float32), axis=(0, 1)),
            jnp.sum(d_values.astype(jnp.float32), axis=(0, 1)),
        ],
        axis=1,
    )
    d_joined_out = jnp.stack([d_queries, d_keys, d_values], axis=3).reshape(n_seqs, n_rows, -1)
    d_joined = jnp.einsum(
        "sbd,sbc->dc", hidden_reduced, d_joined_out, preferred_element_type=jnp.float32
    )
    d_joined = d_joined.reshape(width, n_heads, 3, head_dim)
    d_hidden = jnp.einsum(
        "sbc,dc->sbd",
        d_joined_out,
        combined_weight.reshape(width, -1),
        preferred_element_type=jnp.float32,
    )
    d_hidden = share_sum(d_hidden) + d_resid_one
    small_grads = (
        d_mixer_bias,
        d_down_bias,
        jnp.stack([d_gain_one, d_gain_two]),
        jnp.stack([d_shift_one, d_shift_two]),
    )
    small_grads = lax.psum(
        (
            small_grads[0],
            small_grads[1],
            small_grads[2].astype(jnp.float32),
            small_grads[3].astype(jnp.float32),
        ),
        "tp",
    )
    grads = (
        d_joined,
        d_joined_bias,
        d_mixer,
        small_grads[0],
        d_upward,
        d_up_bias,
        d_down,
        small_grads[1],
        small_grads[2],
        small_grads[3],
    )
    return (d_hidden, grads)


def sum_layer(grads):
    return lax.psum(
        (
            grads[0],
            grads[1],
            grads[2],
            grads[3],
            grads[4],
            grads[5],
            grads[6],
            grads[7],
            grads[8],
            grads[9],
        ),
        "ctx",
    )


def on_device(
    tokens,
    cotangent,
    seq_lengths,
    combined_weight,
    joined_bias,
    attention_out_weight,
    attention_out_bias,
    expand_weight,
    expand_bias,
    contract_weight,
    contract_bias,
    norm_gains,
    norm_shifts,
):
    params = (
        combined_weight,
        joined_bias,
        attention_out_weight,
        attention_out_bias,
        expand_weight,
        expand_bias,
        contract_weight,
        contract_bias,
        norm_gains,
        norm_shifts,
    )
    n_layers = combined_weight.shape[0]
    hidden = tokens.astype(jnp.float32)
    hidden_reduced = tokens
    hidden = take_share(hidden)
    saved = []
    for layer_idx in range(n_layers):
        hidden, kept = forward_layer(
            hidden, hidden_reduced, seq_lengths, *[weight[layer_idx] for weight in params]
        )
        saved.append(kept)
        if layer_idx + 1 < n_layers:
            hidden_reduced = hidden.astype(jnp.bfloat16)
            hidden_reduced = share_gather(hidden_reduced)
    grad_now = cotangent.astype(jnp.float32)
    grad_now = take_share(grad_now)
    collected = []
    for layer_idx in reversed(range(n_layers)):
        grad_now, grads = backward_layer(
            grad_now,
            saved[layer_idx],
            combined_weight[layer_idx],
            attention_out_weight[layer_idx],
            expand_weight[layer_idx],
            contract_weight[layer_idx],
        )
        grads = sum_layer(grads)
        collected.insert(0, grads)
    stacked = tuple((jnp.stack([entry[member] for entry in collected]) for member in range(10)))
    hidden, grad_now = (
        lax.all_gather(hidden, "tp", axis=1, tiled=True),
        lax.all_gather(grad_now, "tp", axis=1, tiled=True),
    )
    return (
        hidden,
        grad_now,
        stacked[0],
        stacked[1],
        stacked[2],
        stacked[3],
        stacked[4],
        stacked[5],
        stacked[6],
        stacked[7],
        stacked[8],
        stacked[9],
    )


def solution(mesh):
    placed = (
        P(None, "ctx", None),
        P(None, "ctx", None),
        P(),
        P(None, None, "tp", None, None),
        P(None, "tp", None, None),
        P(None, "tp", None),
        P(),
        P(None, None, "tp"),
        P(None, "tp"),
        P(None, "tp", None),
        P(),
        P(),
        P(),
    )
    return jax.shard_map(
        on_device,
        mesh=mesh,
        in_specs=placed,
        out_specs=(
            P(None, "ctx", None),
            P(None, "ctx", None),
            P(None, None, "tp", None, None),
            P(None, "tp", None, None),
            P(None, "tp", None),
            P(),
            P(None, None, "tp"),
            P(None, "tp"),
            P(None, "tp", None),
            P(),
            P(),
            P(),
        ),
        check_vma=False,
    )
```

profile of v0, /device:TPU:0, one launch (start us, length us, event | category | flops | bytes accessed | tf_op | source)
XLA Modules:
  0.0 1609.7 jit_solution(18268180588646631589)
XLA Ops:
  12.3 34.3 %all-gather.16.cloned.1.call-done = bf16[8,1024,192]{1,2,0:T(8,128)(2,1)} async-done(((bf16[8,128,192]{1,2,0:T(8,128)(2,1)}), bf16[8,1024,192]{1,2,0:T(8,128)(2,1)}) %all-gather.16.cloned.1.call-update) | async-done | bytes 3145744 | tf_op jit(solution)/shard_map/all_gather | solution.py:73
  55.1 26.9 %all-gather.14.cloned.1.call-done = bf16[8,1024,192]{1,2,0:T(8,128)(2,1)} async-done(((bf16[8,128,192]{1,2,0:T(8,128)(2,1)}), bf16[8,1024,192]{1,2,0:T(8,128)(2,1)}) %all-gather.14.cloned.1.call-update) | async-done | bytes 3145744 | tf_op jit(solution)/shard_map/all_gather | solution.py:74
  81.9 8.5 convolution_convert_fusion.3
  93.7 60.2 %reduce-scatter.13.cloned.1.call-done = f32[8,32,768]{2,1,0:T(8,128)} async-done(((f32[8,128,768]{2,1,0:T(8,128)}), f32[8,32,768]{2,1,0:T(8,128)}) %reduce-scatter.13.cloned.1.call-update) | async-done | bytes 786448 | tf_op jit(solution)/shard_map/reduce_scatter | solution.py:33
  156.7 37.2 %all-gather.18.cloned.1.call-done = bf16[8,128,768]{2,1,0:T(8,128)(2,1)} async-done(((bf16[8,32,768]{2,1,0:T(8,128)(2,1)}), bf16[8,128,768]{2,1,0:T(8,128)(2,1)}) %all-gather.18.cloned.1.call-update) | async-done | bytes 1572880 | tf_op jit(solution)/shard_map/all_gather | solution.py:37
  203.3 58.6 %reduce-scatter.15.cloned.1.call-done = f32[8,32,768]{2,1,0:T(8,128)} async-done(((f32[8,128,768]{2,1,0:T(8,128)}), f32[8,32,768]{2,1,0:T(8,128)}) %reduce-scatter.15.cloned.1.call-update) | async-done | bytes 786448 | tf_op jit(solution)/shard_map/reduce_scatter | solution.py:33
  265.2 36.7 %all-gather.20.cloned.1.call-done = bf16[8,128,768]{2,1,0:T(8,128)(2,1)} async-done(((bf16[8,32,768]{2,1,0:T(8,128)(2,1)}), bf16[8,128,768]{2,1,0:T(8,128)(2,1)}) %all-gather.20.cloned.1.call-update) | async-done | bytes 1572880 | tf_op jit(solution)/shard_map/all_gather | solution.py:37
  309.3 29.5 %all-gather.24.cloned.1.call-done = bf16[8,1024,192]{1,2,0:T(8,128)(2,1)} async-done(((bf16[8,128,192]{1,2,0:T(8,128)(2,1)}), bf16[8,1024,192]{1,2,0:T(8,128)(2,1)}) %all-gather.24.cloned.1.call-update) | async-done | bytes 3145744 | tf_op jit(solution)/shard_map/all_gather | solution.py:73
  347.5 26.6 %all-gather.22.cloned.1.call-done = bf16[8,1024,192]{1,2,0:T(8,128)(2,1)} async-done(((bf16[8,128,192]{1,2,0:T(8,128)(2,1)}), bf16[8,1024,192]{1,2,0:T(8,128)(2,1)}) %all-gather.22.cloned.1.call-update) | async-done | bytes 3145744 | tf_op jit(solution)/shard_map/all_gather | solution.py:74
  384.9 60.3 %reduce-scatter.17.cloned.1.call-done = f32[8,32,768]{2,1,0:T(8,128)} async-done(((f32[8,128,768]{2,1,0:T(8,128)}), f32[8,32,768]{2,1,0:T(8,128)}) %reduce-scatter.17.cloned.1.call-update) | async-done | bytes 786448 | tf_op jit(solution)/shard_map/reduce_scatter | solution.py:33
  448.1 37.2 %all-gather.26.cloned.1.call-done = bf16[8,128,768]{2,1,0:T(8,128)(2,1)} async-done(((bf16[8,32,768]{2,1,0:T(8,128)(2,1)}), bf16[8,128,768]{2,1,0:T(8,128)(2,1)}) %all-gather.26.cloned.1.call-update) | async-done | bytes 1572880 | tf_op jit(solution)/shard_map/all_gather | solution.py:37
  494.3 59.1 %reduce-scatter.19.cloned.1.call-done = f32[8,32,768]{2,1,0:T(8,128)} async-done(((f32[8,128,768]{2,1,0:T(8,128)}), f32[8,32,768]{2,1,0:T(8,128)}) %reduce-scatter.19.cloned.1.call-update) | async-done | bytes 786448 | tf_op jit(solution)/shard_map/reduce_scatter | solution.py:33
  558.8 37.2 %all-gather.30.cloned.1.call-done = bf16[8,128,768]{2,1,0:T(8,128)(2,1)} async-done(((bf16[8,32,768]{2,1,0:T(8,128)(2,1)}), bf16[8,128,768]{2,1,0:T(8,128)(2,1)}) %all-gather.30.cloned.1.call-update) | async-done | bytes 1572880 | tf_op jit(solution)/shard_map/all_gather | solution.py:37
  607.4 59.2 %reduce-scatter.21.cloned.1.call-done = f32[8,32,768]{2,1,0:T(8,128)} async-done(((f32[8,128,768]{2,1,0:T(8,128)}), f32[8,32,768]{2,1,0:T(8,128)}) %reduce-scatter.21.cloned.1.call-update) | async-done | bytes 786448 | tf_op jit(solution)/shard_map/reduce_scatter | solution.py:33
  671.0 37.2 %all-gather.32.cloned.1.call-done = bf16[8,128,768]{2,1,0:T(8,128)(2,1)} async-done(((bf16[8,32,768]{2,1,0:T(8,128)(2,1)}), bf16[8,128,768]{2,1,0:T(8,128)(2,1)}) %all-gather.32.cloned.1.call-update) | async-done | bytes 1572880 | tf_op jit(solution)/shard_map/all_gather | solution.py:37
  710.3 10.3 fusion.75
  752.1 29.3 %reduce-scatter.25.cloned.1.call-done = f32[8,128,192]{1,2,0:T(8,128)} async-done(((f32[8,1024,192]{1,2,0:T(8,128)}), f32[8,128,192]{1,2,0:T(8,128)}) %reduce-scatter.25.cloned.1.call-update) | async-done | bytes 786448 | tf_op jit(solution)/shard_map/reduce_scatter | solution.py:204
  783.3 63.5 %reduce-scatter.23.cloned.1.call-done = f32[8,128,192]{1,2,0:T(8,128)} async-done(((f32[8,1024,192]{1,2,0:T(8,128)}), f32[8,128,192]{1,2,0:T(8,128)}) %reduce-scatter.23.cloned.1.call-update) | async-done | bytes 786448 | tf_op jit(solution)/shard_map/reduce_scatter | solution.py:201
  852.5 60.3 %reduce-scatter.27.cloned.1.call-done = f32[8,32,768]{2,1,0:T(8,128)} async-done(((f32[8,128,768]{2,1,0:T(8,128)}), f32[8,32,768]{2,1,0:T(8,128)}) %reduce-scatter.27.cloned.1.call-update) | async-done | bytes 786448 | tf_op jit(solution)/shard_map/reduce_scatter | solution.py:33
  916.6 37.0 %all-gather.34.cloned.1.call-done = bf16[8,128,768]{2,1,0:T(8,128)(2,1)} async-done(((bf16[8,32,768]{2,1,0:T(8,128)(2,1)}), bf16[8,128,768]{2,1,0:T(8,128)(2,1)}) %all-gather.34.cloned.1.call-update) | async-done | bytes 1572880 | tf_op jit(solution)/shard_map/all_gather | solution.py:37
  964.9 59.2 %reduce-scatter.29.cloned.1.call-done = f32[8,32,768]{2,1,0:T(8,128)} async-done(((f32[8,128,768]{2,1,0:T(8,128)}), f32[8,32,768]{2,1,0:T(8,128)}) %reduce-scatter.29.cloned.1.call-update) | async-done | bytes 786448 | tf_op jit(solution)/shard_map/reduce_scatter | solution.py:33
  1029.1 37.2 %all-gather.36.cloned.1.call-done = bf16[8,128,768]{2,1,0:T(8,128)(2,1)} async-done(((bf16[8,32,768]{2,1,0:T(8,128)(2,1)}), bf16[8,128,768]{2,1,0:T(8,128)(2,1)}) %all-gather.36.cloned.1.call-update) | async-done | bytes 1572880 | tf_op jit(solution)/shard_map/all_gather | solution.py:37
  1068.4 10.2 fusion.78
  1080.5 8.9 multiply_reduce_fusion
  1110.1 29.3 %reduce-scatter.33.cloned.1.call-done = f32[8,128,192]{1,2,0:T(8,128)} async-done(((f32[8,1024,192]{1,2,0:T(8,128)}), f32[8,128,192]{1,2,0:T(8,128)}) %reduce-scatter.33.cloned.1.call-update) | async-done | bytes 786448 | tf_op jit(solution)/shard_map/reduce_scatter | solution.py:204
  1140.7 64.2 %reduce-scatter.31.cloned.1.call-done = f32[8,128,192]{1,2,0:T(8,128)} async-done(((f32[8,1024,192]{1,2,0:T(8,128)}), f32[8,128,192]{1,2,0:T(8,128)}) %reduce-scatter.31.cloned.1.call-update) | async-done | bytes 786448 | tf_op jit(solution)/shard_map/reduce_scatter | solution.py:201
  1232.4 37.5 %reduce-scatter.35.cloned.1.call-done = f32[8,32,768]{2,1,0:T(8,128)} async-done(((f32[8,128,768]{2,1,0:T(8,128)}), f32[8,32,768]{2,1,0:T(8,128)}) %reduce-scatter.35.cloned.1.call-update) | async-done | bytes 786448 | tf_op jit(solution)/shard_map/reduce_scatter | solution.py:33
  1272.2 62.7 %all-gather.28.cloned.1.call-done = f32[8,128,768]{2,1,0:T(8,128)} async-done(((f32[8,32,768]{2,1,0:T(8,128)}), f32[8,128,768]{2,1,0:T(8,128)}) %all-gather.28.cloned.1.call-update) | async-done | bytes 3145744 | tf_op jit(solution)/shard_map/all_gather | solution.py:335
  1335.2 16.9 %all-reduce.2 = (f32[768]{0:T(1024)S(1)}, f32[768]{0:T(1024)S(1)}, f32[768]{0:T(1024)S(1)}, f32[768]{0:T(1024)S(1)}, f32[2,768]{1,0:T(2,128)S(1)}, /*index=5*/f3...) all-reduce(f32[768]{0:T(1024)S(1)} %copy-done.53, ...), channel_id=1, replica_groups=mesh['ctx'=8,'tp'=4] {'tp'}, use_global_device_ids=true, to_apply=%region_48.49 | all-reduce | flops 9216 | bytes 73728 | tf_op jit(solution)/shard_map/psum | solution.py:237
  1352.3 25.3 %all-reduce = (f32[1,3,2,64]{3,2,1,0:T(2,128)S(1)}, f32[1,3,2,64]{3,2,1,0:T(2,128)S(1)}, f32[1,768]{1,0:T(1,128)S(1)}, f32[1,768]{1,0:T(1,128)S(1)}, f32[1,768]{...) all-reduce(f32[1,3,2,64]{3,2,1,0:T(2,128)S(1)} %maximum_bitcast_fus, ...), channel_id=1, replica_groups=mesh['ctx'=8,'tp'=4] {'ctx'}, use_global_device_ids=true, to_apply=%region_41.42 | all-reduce | flops 11520 | bytes 92160 | tf_op jit(solution)/shard_map/psum | solution.py:262
  1381.2 151.4 %all-reduce.5.cloned.1.call-done = (f32[1,768,3,3,64]{1,4,3,2,0:T(8,128)}, f32[1,768,3,3,64]{1,4,3,2,0:T(8,128)}, f32[1,192,768]{2,1,0:T(8,128)}, f32[1,192,768]...) async-done(((f32[1,768,3,3,64]{1,4,3,2,0:T(8,128)}, f32[1,768,3,3,64]{1,4,3,2,0:T(8,128)}, ...) | async-done | bytes 14155792 | tf_op jit(solution)/shard_map/psum | solution.py:262
  1545.8 52.5 %all-gather.38.cloned.1.call-done = f32[8,128,768]{2,1,0:T(8,128)} async-done(((f32[8,32,768]{2,1,0:T(8,128)}), f32[8,128,768]{2,1,0:T(8,128)}) %all-gather.38.cloned.1.call-update) | async-done | bytes 3145744 | tf_op jit(solution)/shard_map/all_gather | solution.py:336
  (377 shorter events, 229.5 us)
Async XLA Ops:
  7.2 39.4 %all-gather.16.cloned.1.call-start = ((), (), s32[]{:S(2)}) async-start(), calls=%async_computation.13 | async-start | bytes 3538944 | tf_op jit(solution)/shard_map/all_gather | solution.py:73
  10.9 71.0 %all-gather.14.cloned.1.call-start = ((), (), s32[]{:S(2)}) async-start(), calls=%async_computation.12 | async-start | bytes 3538944 | tf_op jit(solution)/shard_map/all_gather | solution.py:74
  12.1 141.8 %reduce-scatter.13.cloned.1.call-start = ((), (), s32[]{:S(2)}) async-start(), calls=%async_computation.14 | async-start | bytes 3932160 | tf_op jit(solution)/shard_map/reduce_scatter | solution.py:33
  93.5 100.3 %all-gather.18.cloned.1.call-start = ((), (), s32[]{:S(2)}) async-start(), calls=%async_computation.15 | async-start | bytes 1966080 | tf_op jit(solution)/shard_map/all_gather | solution.py:37
  93.7 168.2 %copy-start.33 = (f32[768]{0:T(1024)}, f32[768]{0:T(1024)S(1)}, u32[]{:S(2)}) copy-start(f32[768]{0:T(1024)S(1)} %get-tuple-element.122) | copy-start | bytes 9220
  93.7 351.5 %copy-start.35 = (f32[768]{0:T(1024)}, f32[768]{0:T(1024)S(1)}, u32[]{:S(2)}) copy-start(f32[768]{0:T(1024)S(1)} %get-tuple-element.123) | copy-start | bytes 9220
  155.6 106.3 %copy-start.37 = (f32[8,32]{1,0:T(8,128)}, f32[8,32]{1,0:T(8,128)S(1)}, u32[]{:S(2)}) copy-start(f32[8,32]{1,0:T(8,128)S(1)} %fusion.87) | copy-start | bytes 3076
  156.6 105.3 %reduce-scatter.15.cloned.1.call-start = ((), (), s32[]{:S(2)}) async-start(), calls=%async_computation.16 | async-start | bytes 3932160 | tf_op jit(solution)/shard_map/reduce_scatter | solution.py:33
  156.7 439.4 %copy-start.70 = (f32[768]{0:T(1024)}, f32[768]{0:T(1024)S(1)}, u32[]{:S(2)}) copy-start(f32[768]{0:T(1024)S(1)} %get-tuple-element.36) | copy-start | bytes 9220
  202.6 99.3 %all-gather.20.cloned.1.call-start = ((), (), s32[]{:S(2)}) async-start(), calls=%async_computation.17 | async-start | bytes 1966080 | tf_op jit(solution)/shard_map/all_gather | solution.py:37
  263.7 181.5 %copy-start.39 = (f32[8,32]{1,0:T(8,128)}, f32[8,32]{1,0:T(8,128)S(1)}, u32[]{:S(2)}) copy-start(f32[8,32]{1,0:T(8,128)S(1)} %fusion.88) | copy-start | bytes 3076
  264.7 74.1 %all-gather.24.cloned.1.call-start = ((), (), s32[]{:S(2)}) async-start(), calls=%async_computation.19 | async-start | bytes 3538944 | tf_op jit(solution)/shard_map/all_gather | solution.py:73
  307.0 67.1 %all-gather.22.cloned.1.call-start = ((), (), s32[]{:S(2)}) async-start(), calls=%async_computation.18 | async-start | bytes 3538944 | tf_op jit(solution)/shard_map/all_gather | solution.py:74
  309.2 136.0 %reduce-scatter.17.cloned.1.call-start = ((), (), s32[]{:S(2)}) async-start(), calls=%async_computation.20 | async-start | bytes 3932160 | tf_op jit(solution)/shard_map/reduce_scatter | solution.py:33
  384.9 100.4 %all-gather.26.cloned.1.call-start = ((), (), s32[]{:S(2)}) async-start(), calls=%async_computation.21 | async-start | bytes 1966080 | tf_op jit(solution)/shard_map/all_gather | solution.py:37
  448.0 105.3 %reduce-scatter.19.cloned.1.call-start = ((), (), s32[]{:S(2)}) async-start(), calls=%async_computation.22 | async-start | bytes 3932160 | tf_op jit(solution)/shard_map/reduce_scatter | solution.py:33
  494.0 102.0 %all-gather.30.cloned.1.call-start = ((), (), s32[]{:S(2)}) async-start(), calls=%async_computation.24 | async-start | bytes 1966080 | tf_op jit(solution)/shard_map/all_gather | solution.py:37
  558.8 107.8 %reduce-scatter.21.cloned.1.call-start = ((), (), s32[]{:S(2)}) async-start(), calls=%async_computation.25 | async-start | bytes 3932160 | tf_op jit(solution)/shard_map/reduce_scatter | solution.py:33
  607.3 100.9 %all-gather.32.cloned.1.call-start = ((), (), s32[]{:S(2)}) async-start(), calls=%async_computation.26 | async-start | bytes 1966080 | tf_op jit(solution)/shard_map/all_gather | solution.py:37
  670.9 110.5 %reduce-scatter.25.cloned.1.call-start = ((), (), s32[]{:S(2)}) async-start(), calls=%async_computation.28 | async-start | bytes 7077888 | tf_op jit(solution)/shard_map/reduce_scatter | solution.py:204
  720.6 126.2 %reduce-scatter.23.cloned.1.call-start = ((), (), s32[]{:S(2)}) async-start(), calls=%async_computation.27 | async-start | bytes 7077888 | tf_op jit(solution)/shard_map/reduce_scatter | solution.py:201
  742.7 170.1 %reduce-scatter.27.cloned.1.call-start = ((), (), s32[]{:S(2)}) async-start(), calls=%async_computation.29 | async-start | bytes 3932160 | tf_op jit(solution)/shard_map/reduce_scatter | solution.py:33
  852.4 101.1 %all-gather.34.cloned.1.call-start = ((), (), s32[]{:S(2)}) async-start(), calls=%async_computation.30 | async-start | bytes 1966080 | tf_op jit(solution)/shard_map/all_gather | solution.py:37
  916.3 107.8 %reduce-scatter.29.cloned.1.call-start = ((), (), s32[]{:S(2)}) async-start(), calls=%async_computation.31 | async-start | bytes 3932160 | tf_op jit(solution)/shard_map/reduce_scatter | solution.py:33
  964.9 101.5 %all-gather.36.cloned.1.call-start = ((), (), s32[]{:S(2)}) async-start(), calls=%async_computation.32 | async-start | bytes 1966080 | tf_op jit(solution)/shard_map/all_gather | solution.py:37
  1029.1 110.4 %reduce-scatter.33.cloned.1.call-start = ((), (), s32[]{:S(2)}) async-start(), calls=%async_computation.34 | async-start | bytes 7077888 | tf_op jit(solution)/shard_map/reduce_scatter | solution.py:204
  1078.7 126.3 %reduce-scatter.31.cloned.1.call-start = ((), (), s32[]{:S(2)}) async-start(), calls=%async_computation.33 | async-start | bytes 7077888 | tf_op jit(solution)/shard_map/reduce_scatter | solution.py:201
  1103.1 166.8 %reduce-scatter.35.cloned.1.call-start = ((), (), s32[]{:S(2)}) async-start(), calls=%async_computation.35 | async-start | bytes 3932160 | tf_op jit(solution)/shard_map/reduce_scatter | solution.py:33
  1209.5 125.3 %all-gather.28.cloned.1.call-start = ((), (), s32[]{:S(2)}) async-start(), calls=%async_computation.23 | async-start | bytes 3932160 | tf_op jit(solution)/shard_map/all_gather | solution.py:335
  1210.1 322.5 %all-reduce.5.cloned.1.call-start = ((), (), s32[]{:S(2)}) async-start(), calls=%async_computation.37 | async-start | bytes 28311552 | tf_op jit(solution)/shard_map/psum | solution.py:262
  1232.3 102.9 %copy-start.52 = (f32[768]{0:T(1024)S(1)}, f32[768]{0:T(1024)}, u32[]{:S(2)}) copy-start(f32[768]{0:T(1024)} %get-tuple-element.13) | copy-start | bytes 9220
  1232.4 366.0 %all-gather.38.cloned.1.call-start = ((), (), s32[]{:S(2)}) async-start(), calls=%async_computation.36 | async-start | bytes 3932160 | tf_op jit(solution)/shard_map/all_gather | solution.py:336
  (86 other events, 2623.3 us)
Sparse Core Ops, SparseCore 0:
  11.1 35.5 all-gather.15
  49.1 32.8 all-gather.13
  93.6 60.2 reduce-scatter.12
  156.7 37.1 all-gather.17
  202.7 59.1 reduce-scatter.14
  264.8 37.0 all-gather.19
  307.1 31.6 all-gather.23
  341.2 32.8 all-gather.21
  385.0 60.2 reduce-scatter.16
  448.1 37.1 all-gather.25
  494.2 59.1 reduce-scatter.18
  558.9 37.0 all-gather.29
  607.4 59.0 reduce-scatter.20
  671.1 37.1 all-gather.31
  720.7 60.6 reduce-scatter.24
  785.0 61.7 reduce-scatter.22
  852.6 60.2 reduce-scatter.26
  916.4 37.0 all-gather.33
  965.0 59.0 reduce-scatter.28
  1029.2 37.1 all-gather.35
  1078.8 60.6 reduce-scatter.32
  1143.2 61.7 reduce-scatter.30
  1209.6 60.2 reduce-scatter.34
  1271.4 63.4 all-gather.27
  1340.7 191.8 all-reduce.4
  1534.7 63.5 all-gather.37
where the time goes:
time: 1620 us; the launch traced here: 1610 us
  waiting for transfers between devices  1290 us (80%)
  matrix products  162 us (10%)
  other arithmetic  73.8 us (5%)
  blocking collectives  42.2 us (3%)
  local copies, waits for them, and re-layouts  28.2 us (2%)
    reduce_scatter x8, waiting for transfers between devices, share_sum(): return lax.psum_scatter(partial_rows, 'tp', scatter_dimension=1, tiled=True)  454 us
    all_gather x7, waiting for transfers between devices, share_gather(): return lax.all_gather(rows_low, 'tp', axis=1, tiled=True)  260 us
    psum x1, waiting for transfers between devices, sum_layer(): lax.psum((grads[0], grads[1], grads[2], grads[3], grads[4], grads[5], gra...  151 us
    reduce_scatter x2, waiting for transfers between devices, backward_layer(): lax.psum_scatter(key_part.reshape(n_seqs, total_len, -1), 'ctx', scatter_...  128 us
    all_gather x2, waiting for transfers between devices, forward_layer(): lax.all_gather(key_rows.reshape(n_seqs, n_rows, -1), 'ctx', axis=1, tiled...  63.8 us
    all_gather x1, waiting for transfers between devices, on_device(): lax.all_gather(hidden, 'tp', axis=1, tiled=True)  62.7 us
    reduce_scatter x2, waiting for transfers between devices, backward_layer(): lax.psum_scatter(value_part.reshape(n_seqs, total_len, -1), 'ctx', scatte...  58.6 us
    all_gather x2, waiting for transfers between devices, forward_layer(): lax.all_gather(value_rows.reshape(n_seqs, n_rows, -1), 'ctx', axis=1, til...  53.5 us
  transfers between devices with their start and end apart: 26, of which 26 were waited for; matrix products, arithmetic and copies ran while one was open for 7% of the time, Pallas kernels for 0%

commit v1 on v0

--- a/solution.py
+++ b/solution.py
@@ -5,6 +5,27 @@
 
 EPS = 1e-12
 MASKED = -1e30
+
+
+def in_order(parts, dim):
+    parts = jnp.moveaxis(parts, 0, dim)
+    shape = parts.shape
+    return parts.reshape(*shape[:dim], shape[dim] * shape[dim + 1], *shape[dim + 2 :])
+
+
+def collected_by_bits(x, axis):
+    size, here = (lax.axis_size(axis), lax.axis_index(axis))
+    tiles, bit = (x[None], 1)
+    while bit < size:
+        other = lax.ppermute(tiles, axis, [(i, i ^ bit) for i in range(size)])
+        low = here & bit == 0
+        tiles = jnp.concatenate([jnp.where(low, tiles, other), jnp.where(low, other, tiles)])
+        bit *= 2
+    return tiles
+
+
+def gather_by_bits(x, axis, dim):
+    return in_order(collected_by_bits(x, axis), dim)
 
 
 def normalize(resid, norm_gain, norm_shift):
@@ -332,7 +353,7 @@
         collected.insert(0, grads)
     stacked = tuple((jnp.stack([entry[member] for entry in collected]) for member in range(10)))
     hidden, grad_now = (
-        lax.all_gather(hidden, "tp", axis=1, tiled=True),
+        gather_by_bits(hidden, "tp", 1),
         lax.all_gather(grad_now, "tp", axis=1, tiled=True),
     )
     return (

time: 1620 us -> 1570 us (0.969)
  waiting for transfers between devices: 1290 us -> 1230 us
    psum x1, waiting for transfers between devices: 151 us -> 74.9 us  [sum_layer(): lax.psum((grads[0], grads[1], grads[2], grads[3], grads[4], grads[5], gra...]
    ppermute x0 -> x2, waiting for transfers between devices: none -> 68 us  [collected_by_bits(): other = lax.ppermute(tiles, axis, [(i, i ^ bit) for i in range(size)])]
    all_gather x1 -> x0, waiting for transfers between devices: 62.7 us -> none  [on_device(): lax.all_gather(hidden, 'tp', axis=1, tiled=True)]
  transfers between devices with their start and end apart: 26 -> 27, of which waited for: 26 -> 26; matrix products, arithmetic and copies ran while one was open for 7% -> 8% of each run, Pallas kernels for 0% -> 0%
where the time goes in v1:
time: 1570 us; the launch traced here: 1560 us
  waiting for transfers between devices  1230 us (78%)
  matrix products  161 us (10%)
  other arithmetic  76.4 us (5%)
  blocking collectives  42 us (3%)
  local copies, waits for them, and re-layouts  31.5 us (2%)
  between operations  15.9 us (1%)
    reduce_scatter x8, waiting for transfers between devices, share_sum(): return lax.psum_scatter(partial_rows, 'tp', scatter_dimension=1, tiled=True)  468 us
    all_gather x7, waiting for transfers between devices, share_gather(): return lax.all_gather(rows_low, 'tp', axis=1, tiled=True)  260 us
    reduce_scatter x2, waiting for transfers between devices, backward_layer(): lax.psum_scatter(key_part.reshape(n_seqs, total_len, -1), 'ctx', scatter_...  127 us
    psum x1, waiting for transfers between devices, sum_layer(): lax.psum((grads[0], grads[1], grads[2], grads[3], grads[4], grads[5], gra...  74.9 us
    ppermute x2, waiting for transfers between devices, collected_by_bits(): other = lax.ppermute(tiles, axis, [(i, i ^ bit) for i in range(size)])  68 us
    all_gather x2, waiting for transfers between devices, forward_layer(): lax.all_gather(key_rows.reshape(n_seqs, n_rows, -1), 'ctx', axis=1, tiled...  63.8 us
    reduce_scatter x2, waiting for transfers between devices, backward_layer(): lax.psum_scatter(value_part.reshape(n_seqs, total_len, -1), 'ctx', scatte...  58.5 us
    all_gather x2, waiting for transfers between devices, forward_layer(): lax.all_gather(value_rows.reshape(n_seqs, n_rows, -1), 'ctx', axis=1, til...  53.5 us
  transfers between devices with their start and end apart: 27, of which 26 were waited for; matrix products, arithmetic and copies ran while one was open for 8% of the time, Pallas kernels for 0%

profile of v1, /device:TPU:0, one launch (start us, length us, event | category | flops | bytes accessed | tf_op | source)
XLA Modules:
  0.0 1561.3 jit_solution(11830162962878777209)
XLA Ops:
  12.3 34.3 %all-gather.15.cloned.1.call-done = bf16[8,1024,192]{1,2,0:T(8,128)(2,1)} async-done(((bf16[8,128,192]{1,2,0:T(8,128)(2,1)}), bf16[8,1024,192]{1,2,0:T(8,128)(2,1)}) %all-gather.15.cloned.1.call-update) | async-done | bytes 3145744 | tf_op jit(solution)/shard_map/all_gather | solution.py:94
  55.1 26.9 %all-gather.13.cloned.1.call-done = bf16[8,1024,192]{1,2,0:T(8,128)(2,1)} async-done(((bf16[8,128,192]{1,2,0:T(8,128)(2,1)}), bf16[8,1024,192]{1,2,0:T(8,128)(2,1)}) %all-gather.13.cloned.1.call-update) | async-done | bytes 3145744 | tf_op jit(solution)/shard_map/all_gather | solution.py:95
  81.9 8.5 convolution_convert_fusion.3
  93.7 60.2 %reduce-scatter.13.cloned.1.call-done = f32[8,32,768]{2,1,0:T(8,128)} async-done(((f32[8,128,768]{2,1,0:T(8,128)}), f32[8,32,768]{2,1,0:T(8,128)}) %reduce-scatter.13.cloned.1.call-update) | async-done | bytes 786448 | tf_op jit(solution)/shard_map/reduce_scatter | solution.py:54
  156.7 37.2 %all-gather.17.cloned.1.call-done = bf16[8,128,768]{2,1,0:T(8,128)(2,1)} async-done(((bf16[8,32,768]{2,1,0:T(8,128)(2,1)}), bf16[8,128,768]{2,1,0:T(8,128)(2,1)}) %all-gather.17.cloned.1.call-update) | async-done | bytes 1572880 | tf_op jit(solution)/shard_map/all_gather | solution.py:58
  203.3 58.6 %reduce-scatter.15.cloned.1.call-done = f32[8,32,768]{2,1,0:T(8,128)} async-done(((f32[8,128,768]{2,1,0:T(8,128)}), f32[8,32,768]{2,1,0:T(8,128)}) %reduce-scatter.15.cloned.1.call-update) | async-done | bytes 786448 | tf_op jit(solution)/shard_map/reduce_scatter | solution.py:54
  264.9 37.0 %all-gather.19.cloned.1.call-done = bf16[8,128,768]{2,1,0:T(8,128)(2,1)} async-done(((bf16[8,32,768]{2,1,0:T(8,128)(2,1)}), bf16[8,128,768]{2,1,0:T(8,128)(2,1)}) %all-gather.19.cloned.1.call-update) | async-done | bytes 1572880 | tf_op jit(solution)/shard_map/all_gather | solution.py:58
  309.3 29.5 %all-gather.23.cloned.1.call-done = bf16[8,1024,192]{1,2,0:T(8,128)(2,1)} async-done(((bf16[8,128,192]{1,2,0:T(8,128)(2,1)}), bf16[8,1024,192]{1,2,0:T(8,128)(2,1)}) %all-gather.23.cloned.1.call-update) | async-done | bytes 3145744 | tf_op jit(solution)/shard_map/all_gather | solution.py:94
  347.5 26.6 %all-gather.21.cloned.1.call-done = bf16[8,1024,192]{1,2,0:T(8,128)(2,1)} async-done(((bf16[8,128,192]{1,2,0:T(8,128)(2,1)}), bf16[8,1024,192]{1,2,0:T(8,128)(2,1)}) %all-gather.21.cloned.1.call-update) | async-done | bytes 3145744 | tf_op jit(solution)/shard_map/all_gather | solution.py:95
  384.9 60.3 %reduce-scatter.17.cloned.1.call-done = f32[8,32,768]{2,1,0:T(8,128)} async-done(((f32[8,128,768]{2,1,0:T(8,128)}), f32[8,32,768]{2,1,0:T(8,128)}) %reduce-scatter.17.cloned.1.call-update) | async-done | bytes 786448 | tf_op jit(solution)/shard_map/reduce_scatter | solution.py:54
  448.1 37.2 %all-gather.25.cloned.1.call-done = bf16[8,128,768]{2,1,0:T(8,128)(2,1)} async-done(((bf16[8,32,768]{2,1,0:T(8,128)(2,1)}), bf16[8,128,768]{2,1,0:T(8,128)(2,1)}) %all-gather.25.cloned.1.call-update) | async-done | bytes 1572880 | tf_op jit(solution)/shard_map/all_gather | solution.py:58
  494.3 59.0 %reduce-scatter.19.cloned.1.call-done = f32[8,32,768]{2,1,0:T(8,128)} async-done(((f32[8,128,768]{2,1,0:T(8,128)}), f32[8,32,768]{2,1,0:T(8,128)}) %reduce-scatter.19.cloned.1.call-update) | async-done | bytes 786448 | tf_op jit(solution)/shard_map/reduce_scatter | solution.py:54
  558.8 37.2 %all-gather.27.cloned.1.call-done = bf16[8,128,768]{2,1,0:T(8,128)(2,1)} async-done(((bf16[8,32,768]{2,1,0:T(8,128)(2,1)}), bf16[8,128,768]{2,1,0:T(8,128)(2,1)}) %all-gather.27.cloned.1.call-update) | async-done | bytes 1572880 | tf_op jit(solution)/shard_map/all_gather | solution.py:58
  607.4 59.2 %reduce-scatter.21.cloned.1.call-done = f32[8,32,768]{2,1,0:T(8,128)} async-done(((f32[8,128,768]{2,1,0:T(8,128)}), f32[8,32,768]{2,1,0:T(8,128)}) %reduce-scatter.21.cloned.1.call-update) | async-done | bytes 786448 | tf_op jit(solution)/shard_map/reduce_scatter | solution.py:54
  671.0 37.2 %all-gather.29.cloned.1.call-done = bf16[8,128,768]{2,1,0:T(8,128)(2,1)} async-done(((bf16[8,32,768]{2,1,0:T(8,128)(2,1)}), bf16[8,128,768]{2,1,0:T(8,128)(2,1)}) %all-gather.29.cloned.1.call-update) | async-done | bytes 1572880 | tf_op jit(solution)/shard_map/all_gather | solution.py:58
  710.3 10.3 fusion.75
  752.2 29.2 %reduce-scatter.25.cloned.1.call-done = f32[8,128,192]{1,2,0:T(8,128)} async-done(((f32[8,1024,192]{1,2,0:T(8,128)}), f32[8,128,192]{1,2,0:T(8,128)}) %reduce-scatter.25.cloned.1.call-update) | async-done | bytes 786448 | tf_op jit(solution)/shard_map/reduce_scatter | solution.py:225
  783.3 63.5 %reduce-scatter.23.cloned.1.call-done = f32[8,128,192]{1,2,0:T(8,128)} async-done(((f32[8,1024,192]{1,2,0:T(8,128)}), f32[8,128,192]{1,2,0:T(8,128)}) %reduce-scatter.23.cloned.1.call-update) | async-done | bytes 786448 | tf_op jit(solution)/shard_map/reduce_scatter | solution.py:222
  852.5 60.3 %reduce-scatter.27.cloned.1.call-done = f32[8,32,768]{2,1,0:T(8,128)} async-done(((f32[8,128,768]{2,1,0:T(8,128)}), f32[8,32,768]{2,1,0:T(8,128)}) %reduce-scatter.27.cloned.1.call-update) | async-done | bytes 786448 | tf_op jit(solution)/shard_map/reduce_scatter | solution.py:54
  916.5 37.0 %all-gather.31.cloned.1.call-done = bf16[8,128,768]{2,1,0:T(8,128)(2,1)} async-done(((bf16[8,32,768]{2,1,0:T(8,128)(2,1)}), bf16[8,128,768]{2,1,0:T(8,128)(2,1)}) %all-gather.31.cloned.1.call-update) | async-done | bytes 1572880 | tf_op jit(solution)/shard_map/all_gather | solution.py:58
  964.9 59.2 %reduce-scatter.29.cloned.1.call-done = f32[8,32,768]{2,1,0:T(8,128)} async-done(((f32[8,128,768]{2,1,0:T(8,128)}), f32[8,32,768]{2,1,0:T(8,128)}) %reduce-scatter.29.cloned.1.call-update) | async-done | bytes 786448 | tf_op jit(solution)/shard_map/reduce_scatter | solution.py:54
  1029.1 37.2 %all-gather.33.cloned.1.call-done = bf16[8,128,768]{2,1,0:T(8,128)(2,1)} async-done(((bf16[8,32,768]{2,1,0:T(8,128)(2,1)}), bf16[8,128,768]{2,1,0:T(8,128)(2,1)}) %all-gather.33.cloned.1.call-update) | async-done | bytes 1572880 | tf_op jit(solution)/shard_map/all_gather | solution.py:58
  1068.4 10.2 fusion.78
  1080.5 8.9 multiply_reduce_fusion
  1110.1 29.3 %reduce-scatter.33.cloned.1.call-done = f32[8,128,192]{1,2,0:T(8,128)} async-done(((f32[8,1024,192]{1,2,0:T(8,128)}), f32[8,128,192]{1,2,0:T(8,128)}) %reduce-scatter.33.cloned.1.call-update) | async-done | bytes 786448 | tf_op jit(solution)/shard_map/reduce_scatter | solution.py:225
  1141.3 63.7 %reduce-scatter.31.cloned.1.call-done = f32[8,128,192]{1,2,0:T(8,128)} async-done(((f32[8,1024,192]{1,2,0:T(8,128)}), f32[8,128,192]{1,2,0:T(8,128)}) %reduce-scatter.31.cloned.1.call-update) | async-done | bytes 786448 | tf_op jit(solution)/shard_map/reduce_scatter | solution.py:222
  1235.0 51.5 %reduce-scatter.35.cloned.1.call-done = f32[8,32,768]{2,1,0:T(8,128)} async-done(((f32[8,128,768]{2,1,0:T(8,128)}), f32[8,32,768]{2,1,0:T(8,128)}) %reduce-scatter.35.cloned.1.call-update) | async-done | bytes 786448 | tf_op jit(solution)/shard_map/reduce_scatter | solution.py:54
  1291.5 68.0 %collective-permute-done.1 = f32[2,8,32,768]{3,2,1,0:T(8,128)} collective-permute-done((f32[2,8,32,768]{3,2,1,0:T(8,128)S(1)}, f32[2,8,32,768]{3,2,1,0:T(8,128)}, u32[]{:S(2)}, u32[]{:S(2)}) %collective-permute-start.1) | collective-permute-done | bytes 1572896 | tf_op jit(solution)/shard_map/ppermute | solution.py:20
  1364.0 18.7 %all-reduce.2 = (f32[768]{0:T(1024)S(1)}, f32[768]{0:T(1024)S(1)}, f32[768]{0:T(1024)S(1)}, f32[768]{0:T(1024)S(1)}, f32[2,768]{1,0:T(2,128)S(1)}, /*index=5*/f3...) all-reduce(f32[768]{0:T(1024)S(1)} %copy-done.52, ...), channel_id=1, replica_groups=mesh['ctx'=8,'tp'=4] {'tp'}, use_global_device_ids=true, to_apply=%region_48.49 | all-reduce | flops 9216 | bytes 73728 | tf_op jit(solution)/shard_map/psum | solution.py:258
  1382.8 23.3 %all-reduce = (f32[1,3,2,64]{3,2,1,0:T(2,128)S(1)}, f32[1,3,2,64]{3,2,1,0:T(2,128)S(1)}, f32[1,768]{1,0:T(1,128)S(1)}, f32[1,768]{1,0:T(1,128)S(1)}, f32[1,768]{...) all-reduce(f32[1,3,2,64]{3,2,1,0:T(2,128)S(1)} %maximum_bitcast_fus, ...), channel_id=1, replica_groups=mesh['ctx'=8,'tp'=4] {'ctx'}, use_global_device_ids=true, to_apply=%region_41.42 | all-reduce | flops 11520 | bytes 92160 | tf_op jit(solution)/shard_map/psum | solution.py:283
  1409.8 74.9 %all-reduce.5.cloned.1.call-done = (f32[1,768,3,3,64]{1,4,3,2,0:T(8,128)}, f32[1,768,3,3,64]{1,4,3,2,0:T(8,128)}, f32[1,192,768]{2,1,0:T(8,128)}, f32[1,192,768]...) async-done(((f32[1,768,3,3,64]{1,4,3,2,0:T(8,128)}, f32[1,768,3,3,64]{1,4,3,2,0:T(8,128)}, ...) | async-done | bytes 14155792 | tf_op jit(solution)/shard_map/psum | solution.py:283
  1497.6 52.9 %all-gather.35.cloned.1.call-done = f32[8,128,768]{2,1,0:T(8,128)} async-done(((f32[8,32,768]{2,1,0:T(8,128)}), f32[8,128,768]{2,1,0:T(8,128)}) %all-gather.35.cloned.1.call-update) | async-done | bytes 3145744 | tf_op jit(solution)/shard_map/all_gather | solution.py:357
  (384 shorter events, 238.2 us)
Async XLA Ops:
  7.2 39.4 %all-gather.15.cloned.1.call-start = ((), (), s32[]{:S(2)}) async-start(), calls=%async_computation.13 | async-start | bytes 3538944 | tf_op jit(solution)/shard_map/all_gather | solution.py:94
  10.9 71.0 %all-gather.13.cloned.1.call-start = ((), (), s32[]{:S(2)}) async-start(), calls=%async_computation.12 | async-start | bytes 3538944 | tf_op jit(solution)/shard_map/all_gather | solution.py:95
  12.1 141.8 %reduce-scatter.13.cloned.1.call-start = ((), (), s32[]{:S(2)}) async-start(), calls=%async_computation.14 | async-start | bytes 3932160 | tf_op jit(solution)/shard_map/reduce_scatter | solution.py:54
  93.5 100.3 %all-gather.17.cloned.1.call-start = ((), (), s32[]{:S(2)}) async-start(), calls=%async_computation.15 | async-start | bytes 1966080 | tf_op jit(solution)/shard_map/all_gather | solution.py:58
  93.7 168.2 %copy-start.32 = (f32[768]{0:T(1024)}, f32[768]{0:T(1024)S(1)}, u32[]{:S(2)}) copy-start(f32[768]{0:T(1024)S(1)} %get-tuple-element.126) | copy-start | bytes 9220
  93.7 351.5 %copy-start.34 = (f32[768]{0:T(1024)}, f32[768]{0:T(1024)S(1)}, u32[]{:S(2)}) copy-start(f32[768]{0:T(1024)S(1)} %get-tuple-element.127) | copy-start | bytes 9220
  155.6 106.3 %copy-start.36 = (f32[8,32]{1,0:T(8,128)}, f32[8,32]{1,0:T(8,128)S(1)}, u32[]{:S(2)}) copy-start(f32[8,32]{1,0:T(8,128)S(1)} %fusion.87) | copy-start | bytes 3076
  156.6 105.3 %reduce-scatter.15.cloned.1.call-start = ((), (), s32[]{:S(2)}) async-start(), calls=%async_computation.16 | async-start | bytes 3932160 | tf_op jit(solution)/shard_map/reduce_scatter | solution.py:54
  156.7 439.4 %copy-start.69 = (f32[768]{0:T(1024)}, f32[768]{0:T(1024)S(1)}, u32[]{:S(2)}) copy-start(f32[768]{0:T(1024)S(1)} %get-tuple-element.36) | copy-start | bytes 9220
  202.6 99.3 %all-gather.19.cloned.1.call-start = ((), (), s32[]{:S(2)}) async-start(), calls=%async_computation.17 | async-start | bytes 1966080 | tf_op jit(solution)/shard_map/all_gather | solution.py:58
  263.7 181.5 %copy-start.38 = (f32[8,32]{1,0:T(8,128)}, f32[8,32]{1,0:T(8,128)S(1)}, u32[]{:S(2)}) copy-start(f32[8,32]{1,0:T(8,128)S(1)} %fusion.88) | copy-start | bytes 3076
  264.7 74.1 %all-gather.23.cloned.1.call-start = ((), (), s32[]{:S(2)}) async-start(), calls=%async_computation.19 | async-start | bytes 3538944 | tf_op jit(solution)/shard_map/all_gather | solution.py:94
  306.9 67.1 %all-gather.21.cloned.1.call-start = ((), (), s32[]{:S(2)}) async-start(), calls=%async_computation.18 | async-start | bytes 3538944 | tf_op jit(solution)/shard_map/all_gather | solution.py:95
  309.2 136.0 %reduce-scatter.17.cloned.1.call-start = ((), (), s32[]{:S(2)}) async-start(), calls=%async_computation.20 | async-start | bytes 3932160 | tf_op jit(solution)/shard_map/reduce_scatter | solution.py:54
  384.8 100.4 %all-gather.25.cloned.1.call-start = ((), (), s32[]{:S(2)}) async-start(), calls=%async_computation.21 | async-start | bytes 1966080 | tf_op jit(solution)/shard_map/all_gather | solution.py:58
  448.0 105.3 %reduce-scatter.19.cloned.1.call-start = ((), (), s32[]{:S(2)}) async-start(), calls=%async_computation.22 | async-start | bytes 3932160 | tf_op jit(solution)/shard_map/reduce_scatter | solution.py:54
  494.0 102.0 %all-gather.27.cloned.1.call-start = ((), (), s32[]{:S(2)}) async-start(), calls=%async_computation.23 | async-start | bytes 1966080 | tf_op jit(solution)/shard_map/all_gather | solution.py:58
  558.8 107.8 %reduce-scatter.21.cloned.1.call-start = ((), (), s32[]{:S(2)}) async-start(), calls=%async_computation.24 | async-start | bytes 3932160 | tf_op jit(solution)/shard_map/reduce_scatter | solution.py:54
  607.3 100.9 %all-gather.29.cloned.1.call-start = ((), (), s32[]{:S(2)}) async-start(), calls=%async_computation.25 | async-start | bytes 1966080 | tf_op jit(solution)/shard_map/all_gather | solution.py:58
  670.9 110.5 %reduce-scatter.25.cloned.1.call-start = ((), (), s32[]{:S(2)}) async-start(), calls=%async_computation.27 | async-start | bytes 7077888 | tf_op jit(solution)/shard_map/reduce_scatter | solution.py:225
  720.6 126.2 %reduce-scatter.23.cloned.1.call-start = ((), (), s32[]{:S(2)}) async-start(), calls=%async_computation.26 | async-start | bytes 7077888 | tf_op jit(solution)/shard_map/reduce_scatter | solution.py:222
  742.9 170.0 %reduce-scatter.27.cloned.1.call-start = ((), (), s32[]{:S(2)}) async-start(), calls=%async_computation.28 | async-start | bytes 3932160 | tf_op jit(solution)/shard_map/reduce_scatter | solution.py:54
  852.4 101.1 %all-gather.31.cloned.1.call-start = ((), (), s32[]{:S(2)}) async-start(), calls=%async_computation.29 | async-start | bytes 1966080 | tf_op jit(solution)/shard_map/all_gather | solution.py:58
  916.3 107.8 %reduce-scatter.29.cloned.1.call-start = ((), (), s32[]{:S(2)}) async-start(), calls=%async_computation.30 | async-start | bytes 3932160 | tf_op jit(solution)/shard_map/reduce_scatter | solution.py:54
  964.9 101.5 %all-gather.33.cloned.1.call-start = ((), (), s32[]{:S(2)}) async-start(), calls=%async_computation.31 | async-start | bytes 1966080 | tf_op jit(solution)/shard_map/all_gather | solution.py:58
  1029.1 110.4 %reduce-scatter.33.cloned.1.call-start = ((), (), s32[]{:S(2)}) async-start(), calls=%async_computation.33 | async-start | bytes 7077888 | tf_op jit(solution)/shard_map/reduce_scatter | solution.py:225
  1078.6 126.3 %reduce-scatter.31.cloned.1.call-start = ((), (), s32[]{:S(2)}) async-start(), calls=%async_computation.32 | async-start | bytes 7077888 | tf_op jit(solution)/shard_map/reduce_scatter | solution.py:222
  1103.1 183.4 %reduce-scatter.35.cloned.1.call-start = ((), (), s32[]{:S(2)}) async-start(), calls=%async_computation.34 | async-start | bytes 3932160 | tf_op jit(solution)/shard_map/reduce_scatter | solution.py:54
  1209.5 275.1 %all-reduce.5.cloned.1.call-start = ((), (), s32[]{:S(2)}) async-start(), calls=%async_computation.36 | async-start | bytes 28311552 | tf_op jit(solution)/shard_map/psum | solution.py:283
  1232.4 318.1 %all-gather.35.cloned.1.call-start = ((), (), s32[]{:S(2)}) async-start(), calls=%async_computation.35 | async-start | bytes 3932160 | tf_op jit(solution)/shard_map/all_gather | solution.py:357
  1233.5 55.2 %collective-permute-start = (f32[1,8,32,768]{3,2,1,0:T(8,128)S(1)}, f32[1,8,32,768]{3,2,1,0:T(8,128)S(1)}, u32[]{:S(2)}, u32[]{:S(2)}) collective-permute-start(f32[1,8,32,768]{3,2,1,0:T(8,128)S(1)} %copy-done.13), channel_id=1, source_target_pairs={{0,1},{1,0},{2,3},{3,2},{4,5},{5,4},{6,7},{7,6},{8,9},{9,8},{10,11... | collective-permute-start | bytes 2359304 | tf_op jit(solution)/shard_map/ppermute | solution.py:20
  1289.0 70.6 %collective-permute-start.1 = (f32[2,8,32,768]{3,2,1,0:T(8,128)S(1)}, f32[2,8,32,768]{3,2,1,0:T(8,128)}, u32[]{:S(2)}, u32[]{:S(2)}) collective-permute-start(f32[2,8,32,768]{3,2,1,0:T(8,128)S(1)} %pad_maximum_fusion.3), channel_id=1, source_target_pairs={{0,2},{1,3},{2,0},{3,1},{4,6},{5,7},{6,4},{7,5},{8,10},{9,11},{10,... | collective-permute-start | bytes 4718600 | tf_op jit(solution)/shard_map/ppermute | solution.py:20
  (88 other events, 1388.4 us)
Sparse Core Ops, SparseCore 0:
  11.1 35.5 all-gather.14
  49.1 32.8 all-gather.12
  93.6 60.2 reduce-scatter.12
  156.7 37.1 all-gather.16
  202.7 59.1 reduce-scatter.14
  264.8 37.0 all-gather.18
  307.1 31.6 all-gather.22
  341.2 32.8 all-gather.20
  385.0 60.2 reduce-scatter.16
  448.1 37.1 all-gather.24
  494.2 59.1 reduce-scatter.18
  558.9 37.0 all-gather.26
  607.4 59.0 reduce-scatter.20
  671.1 37.1 all-gather.28
  720.7 60.6 reduce-scatter.24
  785.0 61.7 reduce-scatter.22
  852.6 60.2 reduce-scatter.26
  916.4 37.0 all-gather.30
  965.0 59.0 reduce-scatter.28
  1029.2 37.1 all-gather.32
  1078.8 60.6 reduce-scatter.32
  1143.2 61.7 reduce-scatter.30
  1209.6 76.7 reduce-scatter.34
  1292.2 192.4 all-reduce.4
  1486.9 63.5 all-gather.34
